TPU v7x, 32 devices: a whole 2x2x4 slice. The times are simulated.
32 devices in a mesh: inv: 2 (over x), azim: 16 (over z, y, core).
Axes of the slice: x: 2, y: 2, z: 4, core: 2. Of those that a mesh axis runs over, the one named last changes fastest.
Arguments:
- forward_field: float32 [8, 64, 8, 1024], P('inv', 'azim'), parts along dimension 0, may hold values from -6 to 6
- conductivity: float32 [64, 16, 1024], P('azim', 'inv'), parts along dimension 1, may hold values from 0.1 to 10
- conductivity_mid: float32 [32, 8, 512], P('azim', 'inv'), parts along dimension 1, may hold values from 0.1 to 10
- conductivity_coarse: float32 [16, 4, 256], P('azim', 'inv'), parts along dimension 1, may hold values from 0.1 to 10
- receiver_cells: int32 [16, 8192], P('azim', 'inv'), parts along dimension 1, may hold values from 0 to 32767
- receiver_weights: float32 [8, 16, 4096], P('inv', 'azim'), parts along dimension 0, may hold values from -24 to 24
Outputs:
- adjoint_field: float32 [8, 64, 8, 1024], P('inv', 'azim'), parts along dimension 0
- gradient: float32 [64, 16, 1024], P('azim', 'inv'), parts along dimension 1
There are 2 independent parts, one for each index of `inv`. A program takes and returns all parts, laid end to end along the dimension named above; each array names one. Nothing has to cross between parts.
Inputs may be any that keep to these rules, and one draw needn't show every extreme that they name: `receiver_cells`: each entry is a cell of the azimuth block of the device that holds it; several receivers may share a cell.
All inputs are finite; a program needn't handle non-finite values.
Results may differ from a plain program's by a relative error of at most 0.0001.
Values sent between devices are 32-bit elements; how exact they have to be, the bound alone decides.
A program may use at most 128 MiB of HBM per device.

v0:
```python
import math

import jax
import jax.numpy as jnp
from jax import lax
from jax.sharding import PartitionSpec as P

SWEEPS = 2
COARSE_SWEEPS = 4
CYCLES = 2


OMEGA = 0.7
BETA = 0.05


def padded_2(block, sides, width):
    for axis, dim in sides:
        count = lax.axis_size(axis)
        forward = [(i, i + 1) for i in range(count - 1)]
        forward.append((count - 1, 0))
        backward = [(target, source) for source, target in forward]
        low = lax.ppermute(
            lax.slice_in_dim(block, block.shape[dim] - width, None, axis=dim), axis, forward
        )
        high = lax.ppermute(lax.slice_in_dim(block, 0, width, axis=dim), axis, backward)
        block = jnp.concatenate([low, block, high], axis=dim)
    return block


def geometry(spacing, radial, total_azim):
    inner = total_azim // 6
    theta = 2.0 * math.pi * spacing / total_azim
    index = jnp.arange(radial, dtype=jnp.float32)
    centre = inner + spacing * (index + 0.5)
    outer = inner + spacing * (index + 1.0)
    return (centre, outer, theta)


def coefficients(sigma_ext, spacing, total_azim):
    centre, outer, theta = geometry(spacing, sigma_ext.shape[-1], total_azim)
    middle = sigma_ext[1:-1]
    radial_faces = outer[:-1] * theta * 0.5 * (middle[:, :, :-1] + middle[:, :, 1:])
    depth_faces = centre * theta * 0.5 * (middle[:, :-1, :] + middle[:, 1:, :])
    azim_faces = spacing * spacing / (centre * theta) * 0.5 * (sigma_ext[:-1] + sigma_ext[1:])
    radial_high = jnp.pad(radial_faces, ((0, 0), (0, 0), (0, 1)))
    radial_low = jnp.pad(radial_faces, ((0, 0), (0, 0), (1, 0)))
    depth_high = jnp.pad(depth_faces, ((0, 0), (0, 1), (0, 0)))
    depth_low = jnp.pad(depth_faces, ((0, 0), (1, 0), (0, 0)))
    diagonal = (
        radial_high
        + radial_low
        + depth_high
        + depth_low
        + azim_faces[:-1]
        + azim_faces[1:]
        + BETA * spacing * spacing * theta * centre * middle
    )
    return (diagonal, azim_faces, radial_high, radial_low, depth_high, depth_low)


def operate(padded, coeffs):
    diagonal, azim_faces, radial_high, radial_low, depth_high, depth_low = coeffs
    middle = padded[:, 1:-1]
    edge_radial = jnp.zeros_like(middle[:, :, :, :1])
    edge_depth = jnp.zeros_like(middle[:, :, :1, :])
    outward = jnp.concatenate([middle[:, :, :, 1:], edge_radial], axis=3)
    inward = jnp.concatenate([edge_radial, middle[:, :, :, :-1]], axis=3)
    deeper = jnp.concatenate([middle[:, :, 1:, :], edge_depth], axis=2)
    higher = jnp.concatenate([edge_depth, middle[:, :, :-1, :]], axis=2)
    near = (
        azim_faces[:-1] * padded[:, :-2]
        + azim_faces[1:] * padded[:, 2:]
        + radial_high * outward
        + radial_low * inward
        + depth_high * deeper
        + depth_low * higher
    )
    return (diagonal * middle - near, diagonal)


def sweep(padded, right, coeffs):
    image, own_diag = operate(padded, coeffs)
    return padded[:, 1:-1] + OMEGA * ((right - image) / own_diag)


def restrict(field):
    shape = field.shape
    grouped = field.reshape(shape[0], shape[1] // 2, 2, shape[2] // 2, 2, shape[3] // 2, 2)
    return grouped.sum(axis=(2, 4, 6))


def prolong(field):
    return jnp.repeat(jnp.repeat(jnp.repeat(field, 2, axis=1), 2, axis=2), 2, axis=3)


def sensitivity(forward_pad, adjoint_pad, total_azim):
    centre, outer, theta = geometry(1, forward_pad.shape[-1], total_azim)
    forward_mid = forward_pad[:, 1:-1]
    adjoint_mid = adjoint_pad[:, 1:-1]
    azim = jnp.sum(
        (forward_pad[:, 1:] - forward_pad[:, :-1]) * (adjoint_pad[:, 1:] - adjoint_pad[:, :-1]),
        axis=0,
    )
    radial = jnp.sum(
        (forward_mid[..., 1:] - forward_mid[..., :-1])
        * (adjoint_mid[..., 1:] - adjoint_mid[..., :-1]),
        axis=0,
    )
    radial = radial * (outer[:-1] * theta)
    depth = jnp.sum(
        (forward_mid[:, :, 1:] - forward_mid[:, :, :-1])
        * (adjoint_mid[:, :, 1:] - adjoint_mid[:, :, :-1]),
        axis=0,
    )
    own = jnp.sum(forward_mid * adjoint_mid, axis=0)
    total = (
        0.5 / (centre * theta) * (azim[:-1] + azim[1:])
        + 0.5
        * (jnp.pad(radial, ((0, 0), (0, 0), (1, 0))) + jnp.pad(radial, ((0, 0), (0, 0), (0, 1))))
        + 0.5
        * centre
        * theta
        * (jnp.pad(depth, ((0, 0), (1, 0), (0, 0))) + jnp.pad(depth, ((0, 0), (0, 1), (0, 0))))
        + BETA * theta * centre * own
    )
    return -total


def field_rims(field):
    return padded_2(field, (("azim", 1),), 1)


def conductivity_halo(sigma, width):
    return padded_2(sigma, (("azim", 0),), width)


def relax(field, right, coeffs, count, from_zero):
    for turn in range(count):
        if from_zero and turn == 0:
            field = OMEGA * (right / coeffs[0])
        else:
            field = sweep(field_rims(field), right, coeffs)
    return field


def smooth(field, right, coeffs):
    return relax(field, right, coeffs, SWEEPS, False)


def coarse_solve(right_coarse, coarse):
    return relax(jnp.zeros_like(right_coarse), right_coarse, coarse, COARSE_SWEEPS, True)


def vcycle(field, right, levels, first_cycle):
    fine, middle_level, coarse = levels
    if first_cycle:
        field = relax(field, right, fine, SWEEPS, True)
    else:
        field = smooth(field, right, fine)
    image, unused = operate(field_rims(field), fine)
    right_mid = restrict(right - image)
    mid_field = relax(jnp.zeros_like(right_mid), right_mid, middle_level, SWEEPS, True)
    image_mid, unused = operate(field_rims(mid_field), middle_level)
    right_coarse = restrict(right_mid - image_mid)
    coarse_field = coarse_solve(right_coarse, coarse)
    mid_field = smooth(mid_field + prolong(coarse_field), right_mid, middle_level)
    return smooth(field + prolong(mid_field), right, fine)


def local(
    forward_field,
    conductivity,
    conductivity_mid,
    conductivity_coarse,
    receiver_cells,
    receiver_weights,
):
    sources = forward_field.shape[0]
    total_azim = forward_field.shape[1] * lax.axis_size("azim")
    width = 1
    fine = coefficients(conductivity_halo(conductivity, width), 1, total_azim)
    middle_level = coefficients(conductivity_halo(conductivity_mid, width), 2, total_azim)
    coarse = coefficients(conductivity_halo(conductivity_coarse, 1), 4, total_azim)
    levels = (fine, middle_level, coarse)
    shape = forward_field.shape
    cells_dev = shape[1] * shape[2] * shape[3]
    source = (
        jnp.zeros((sources, cells_dev), jnp.float32)
        .at[:, receiver_cells.reshape(-1)]
        .add(receiver_weights.reshape(sources, -1))
    )
    source = source.reshape(shape)
    adjoint = jnp.zeros_like(source)
    for cycle in range(CYCLES):
        adjoint = vcycle(adjoint, source, levels, cycle == 0)
    stacked = field_rims(jnp.concatenate([forward_field, adjoint], axis=0))
    gradient = sensitivity(stacked[:sources], stacked[sources:], total_azim)
    return (adjoint, gradient)


def solution(mesh):
    placed = (
        P("inv", "azim", None, None),
        P("azim", "inv", None),
        P("azim", "inv", None),
        P("azim", "inv", None),
        P("azim", "inv"),
        P("inv", "azim", None),
    )
    return jax.shard_map(
        local,
        mesh=mesh,
        in_specs=placed,
        out_specs=(P("inv", "azim", None, None), P("azim", "inv", None)),
        check_vma=False,
    )
```

profile of v0, /device:TPU:0, one launch (start us, length us, event | category | flops | bytes accessed | tf_op | source)
XLA Modules:
  0.0 396.1 jit_solution(11652256174910317880)
XLA Ops:
  1.1 5.1 %collective-permute-start.13 = (f32[1,2,256]{2,1,0:T(2,128)}, f32[1,2,256]{2,1,0:T(2,128)S(1)}, u32[]{:S(2)}, u32[]{:S(2)}) collective-permute-start(f32[1,2,256]{2,1,0:T(2,128)} %param.9), channel_id=1, source_target_pairs={{1,0},{2,1},{3,2},{4,3},{5,4},{6,5},{7,6},{8,7},{9,8},{10,9},{11,1... | collective-permute-start | bytes 6152 | tf_op jit(solution)/shard_map/ppermute | solution.py:26
  23.8 29.5 %scatter_custom_fusion = f32[4,32768]{0,1:T(8,128)} fusion(s32[4096]{0:T(1024)S(1)} %bitcast.120, f32[4096,4]{1,0:T(8,128)} %copy.377, f32[]{:T(128)} %constant.19.clone.1), kind=kCustom, calls=%fused_computation.1 | custom fusion | flops 16384 | bytes 524800 | tf_op jit(solution)/shard_map/scatter-add | solution.py:191
  53.4 10.0 %copy.421 = f32[4,4,8,1024]{3,2,1,0:T(8,128)S(1)} copy(f32[4,4,8,1024]{0,3,2,1:T(8,128)} %bitcast.106) | data formatting | bytes 1048576 | tf_op jit(solution)/shard_map/reshape | solution.py:193
  78.1 4.5 %collective-permute-start.5 = (f32[4,1,8,1024]{3,2,1,0:T(8,128)S(1)}, f32[4,1,8,1024]{3,2,1,0:T(8,128)S(1)}, u32[]{:S(2)}, u32[]{:S(2)}) collective-permute-start(f32[4,1,8,1024]{3,2,1,0:T(8,128)S(1)} %get-tuple-element.71), channel_id=1, source_target_pairs={{1,0},{2,1},{3,2},{4,3},{5,4},{6,5},{7,6},{8,7},{9,8},{10,9},{11,1... | collective-permute-start | bytes 393224 | tf_op jit(solution)/shard_map/ppermute | solution.py:26
  85.8 8.7 %copy.380 = f32[4,4,8,1024]{0,3,2,1:T(8,128)} copy(f32[4,4,8,1024]{3,2,1,0:T(8,128)S(1)} %fusion.84) | data formatting | bytes 1048576 | tf_op jit(solution)/shard_map/sub | solution.py:162
  94.4 24.6 %reduce_sum.90 = f32[4,2,4,512]{0,3,2,1:T(8,128)} reduce(f32[4,2,2,4,2,512,2]{0,6,5,4,3,2,1:T(2,128)} %bitcast.107, f32[]{:T(128)} %constant.19.clone.1), dimensions={2,4,6}, to_apply=%region_1.2 | reduce | flops 114688 | bytes 589828 | tf_op jit(solution)/shard_map/reduce_sum | solution.py:90
  121.5 4.6 %collective-permute-start.9 = (f32[4,1,4,512]{3,2,1,0:T(4,128)S(1)}, f32[4,1,4,512]{3,2,1,0:T(4,128)S(1)}, u32[]{:S(2)}, u32[]{:S(2)}) collective-permute-start(f32[4,1,4,512]{3,2,1,0:T(4,128)S(1)} %get-tuple-element.157), channel_id=1, source_target_pairs={{1,0},{2,1},{3,2},{4,3},{5,4},{6,5},{7,6},{8,7},{9,8},{10,9},{11,1... | collective-permute-start | bytes 98312 | tf_op jit(solution)/shard_map/ppermute | solution.py:26
  127.9 4.7 %collective-permute-start.11 = (f32[4,1,4,512]{3,2,1,0:T(4,128)S(1)}, f32[4,1,4,512]{3,2,1,0:T(4,128)S(1)}, u32[]{:S(2)}, u32[]{:S(2)}) collective-permute-start(f32[4,1,4,512]{3,2,1,0:T(4,128)S(1)} %get-tuple-element.147), channel_id=1, source_target_pairs={{1,0},{2,1},{3,2},{4,3},{5,4},{6,5},{7,6},{8,7},{9,8},{10,9},{11,1... | collective-permute-start | bytes 98312 | tf_op jit(solution)/shard_map/ppermute | solution.py:26
  138.3 4.5 %collective-permute-start.15 = (f32[4,1,2,256]{0,3,2,1:T(8,128)S(1)}, f32[4,1,2,256]{0,3,2,1:T(8,128)S(1)}, u32[]{:S(2)}, u32[]{:S(2)}) collective-permute-start(f32[4,1,2,256]{0,3,2,1:T(8,128)S(1)} %broadcast_multiply_fusion.2), channel_id=1, source_target_pairs={{1,0},{2,1},{3,2},{4,3},{5,4},{6,5},{7,6},{8,7},{9,8},{10,9},{11,1... | collective-permute-start | bytes 24584 | tf_op jit(solution)/shard_map/ppermute | solution.py:26
  157.8 4.5 %collective-permute-start.19 = (f32[4,1,2,256]{0,3,2,1:T(8,128)S(1)}, f32[4,1,2,256]{0,3,2,1:T(8,128)S(1)}, u32[]{:S(2)}, u32[]{:S(2)}) collective-permute-start(f32[4,1,2,256]{0,3,2,1:T(8,128)S(1)} %fusion.111), channel_id=1, source_target_pairs={{1,0},{2,1},{3,2},{4,3},{5,4},{6,5},{7,6},{8,7},{9,8},{10,9},{11,1... | collective-permute-start | bytes 24584 | tf_op jit(solution)/shard_map/ppermute | solution.py:26
  171.5 4.6 %collective-permute-start.21 = (f32[4,1,4,512]{3,2,1,0:T(4,128)S(1)}, f32[4,1,4,512]{3,2,1,0:T(4,128)S(1)}, u32[]{:S(2)}, u32[]{:S(2)}) collective-permute-start(f32[4,1,4,512]{3,2,1,0:T(4,128)S(1)} %get-tuple-element.145), channel_id=1, source_target_pairs={{1,0},{2,1},{3,2},{4,3},{5,4},{6,5},{7,6},{8,7},{9,8},{10,9},{11,1... | collective-permute-start | bytes 98312 | tf_op jit(solution)/shard_map/ppermute | solution.py:26
  178.9 4.6 %collective-permute-start.23 = (f32[4,1,4,512]{3,2,1,0:T(4,128)S(1)}, f32[4,1,4,512]{3,2,1,0:T(4,128)S(1)}, u32[]{:S(2)}, u32[]{:S(2)}) collective-permute-start(f32[4,1,4,512]{3,2,1,0:T(4,128)S(1)} %get-tuple-element.139), channel_id=1, source_target_pairs={{1,0},{2,1},{3,2},{4,3},{5,4},{6,5},{7,6},{8,7},{9,8},{10,9},{11,1... | collective-permute-start | bytes 98312 | tf_op jit(solution)/shard_map/ppermute | solution.py:26
  188.2 6.7 %broadcast_in_dim.42 = f32[4,4,8,512,2]{2,4,3,1,0:T(2,128)} broadcast(f32[4,4,8,512]{2,3,1,0:T(8,128)} %copy.392), dimensions={0,1,2,3} | broadcast | bytes 786432 | tf_op jit(solution)/shard_map/broadcast_in_dim | solution.py:94
  194.9 5.1 %copy.393 = f32[4,4,8,1024]{3,2,1,0:T(8,128)S(1)} copy(f32[4,4,8,1024]{2,3,1,0:T(8,128)} %bitcast.109) | data formatting | bytes 1048576 | tf_op jit(solution)/shard_map/reshape | solution.py:94
  200.4 4.5 %collective-permute-start.25 = (f32[4,1,8,1024]{3,2,1,0:T(8,128)S(1)}, f32[4,1,8,1024]{3,2,1,0:T(8,128)S(1)}, u32[]{:S(2)}, u32[]{:S(2)}) collective-permute-start(f32[4,1,8,1024]{3,2,1,0:T(8,128)S(1)} %get-tuple-element.65), channel_id=1, source_target_pairs={{1,0},{2,1},{3,2},{4,3},{5,4},{6,5},{7,6},{8,7},{9,8},{10,9},{11,1... | collective-permute-start | bytes 393224 | tf_op jit(solution)/shard_map/ppermute | solution.py:26
  208.4 4.5 %collective-permute-start.27 = (f32[4,1,8,1024]{3,2,1,0:T(8,128)S(1)}, f32[4,1,8,1024]{3,2,1,0:T(8,128)S(1)}, u32[]{:S(2)}, u32[]{:S(2)}) collective-permute-start(f32[4,1,8,1024]{3,2,1,0:T(8,128)S(1)} %get-tuple-element.59), channel_id=1, source_target_pairs={{1,0},{2,1},{3,2},{4,3},{5,4},{6,5},{7,6},{8,7},{9,8},{10,9},{11,1... | collective-permute-start | bytes 393224 | tf_op jit(solution)/shard_map/ppermute | solution.py:26
  216.5 4.5 %collective-permute-start.29 = (f32[4,1,8,1024]{3,2,1,0:T(8,128)S(1)}, f32[4,1,8,1024]{3,2,1,0:T(8,128)S(1)}, u32[]{:S(2)}, u32[]{:S(2)}) collective-permute-start(f32[4,1,8,1024]{3,2,1,0:T(8,128)S(1)} %get-tuple-element.53), channel_id=1, source_target_pairs={{1,0},{2,1},{3,2},{4,3},{5,4},{6,5},{7,6},{8,7},{9,8},{10,9},{11,1... | collective-permute-start | bytes 393224 | tf_op jit(solution)/shard_map/ppermute | solution.py:26
  224.6 4.5 %collective-permute-start.31 = (f32[4,1,8,1024]{3,2,1,0:T(8,128)S(1)}, f32[4,1,8,1024]{3,2,1,0:T(8,128)S(1)}, u32[]{:S(2)}, u32[]{:S(2)}) collective-permute-start(f32[4,1,8,1024]{3,2,1,0:T(8,128)S(1)} %get-tuple-element.47), channel_id=1, source_target_pairs={{1,0},{2,1},{3,2},{4,3},{5,4},{6,5},{7,6},{8,7},{9,8},{10,9},{11,1... | collective-permute-start | bytes 393224 | tf_op jit(solution)/shard_map/ppermute | solution.py:26
  232.6 14.8 %collective-permute-start.33 = (f32[4,1,8,1024]{3,2,1,0:T(8,128)S(1)}, f32[4,1,8,1024]{3,2,1,0:T(8,128)S(1)}, u32[]{:S(2)}, u32[]{:S(2)}) collective-permute-start(f32[4,1,8,1024]{3,2,1,0:T(8,128)S(1)} %get-tuple-element.41), channel_id=1, source_target_pairs={{1,0},{2,1},{3,2},{4,3},{5,4},{6,5},{7,6},{8,7},{9,8},{10,9},{11,1... | collective-permute-start | bytes 393224 | tf_op jit(solution)/shard_map/ppermute | solution.py:26
  250.4 8.7 %copy.394 = f32[4,4,8,1024]{0,3,2,1:T(8,128)} copy(f32[4,4,8,1024]{3,2,1,0:T(8,128)S(1)} %fusion.35) | data formatting | bytes 1048576 | tf_op jit(solution)/shard_map/sub | solution.py:162
  259.0 24.6 %reduce_sum.95 = f32[4,2,4,512]{0,3,2,1:T(8,128)} reduce(f32[4,2,2,4,2,512,2]{0,6,5,4,3,2,1:T(2,128)} %bitcast.108, f32[]{:T(128)} %constant.19.clone.1), dimensions={2,4,6}, to_apply=%region_4.5 | reduce | flops 114688 | bytes 589828 | tf_op jit(solution)/shard_map/reduce_sum | solution.py:90
  286.1 4.6 %collective-permute-start.35 = (f32[4,1,4,512]{3,2,1,0:T(4,128)S(1)}, f32[4,1,4,512]{3,2,1,0:T(4,128)S(1)}, u32[]{:S(2)}, u32[]{:S(2)}) collective-permute-start(f32[4,1,4,512]{3,2,1,0:T(4,128)S(1)} %get-tuple-element.133), channel_id=1, source_target_pairs={{1,0},{2,1},{3,2},{4,3},{5,4},{6,5},{7,6},{8,7},{9,8},{10,9},{11,1... | collective-permute-start | bytes 98312 | tf_op jit(solution)/shard_map/ppermute | solution.py:26
  292.6 4.5 %collective-permute-start.37 = (f32[4,1,4,512]{3,2,1,0:T(4,128)S(1)}, f32[4,1,4,512]{3,2,1,0:T(4,128)S(1)}, u32[]{:S(2)}, u32[]{:S(2)}) collective-permute-start(f32[4,1,4,512]{3,2,1,0:T(4,128)S(1)} %get-tuple-element.123), channel_id=1, source_target_pairs={{1,0},{2,1},{3,2},{4,3},{5,4},{6,5},{7,6},{8,7},{9,8},{10,9},{11,1... | collective-permute-start | bytes 98312 | tf_op jit(solution)/shard_map/ppermute | solution.py:26
  312.7 4.6 %collective-permute-start.41 = (f32[4,1,2,256]{0,3,2,1:T(8,128)S(1)}, f32[4,1,2,256]{0,3,2,1:T(8,128)S(1)}, u32[]{:S(2)}, u32[]{:S(2)}) collective-permute-start(f32[4,1,2,256]{0,3,2,1:T(8,128)S(1)} %fusion.98), channel_id=1, source_target_pairs={{1,0},{2,1},{3,2},{4,3},{5,4},{6,5},{7,6},{8,7},{9,8},{10,9},{11,1... | collective-permute-start | bytes 24584 | tf_op jit(solution)/shard_map/ppermute | solution.py:26
  322.1 4.5 %collective-permute-start.43 = (f32[4,1,2,256]{0,3,2,1:T(8,128)S(1)}, f32[4,1,2,256]{0,3,2,1:T(8,128)S(1)}, u32[]{:S(2)}, u32[]{:S(2)}) collective-permute-start(f32[4,1,2,256]{0,3,2,1:T(8,128)S(1)} %fusion.101), channel_id=1, source_target_pairs={{1,0},{2,1},{3,2},{4,3},{5,4},{6,5},{7,6},{8,7},{9,8},{10,9},{11,1... | collective-permute-start | bytes 24584 | tf_op jit(solution)/shard_map/ppermute | solution.py:26
  335.9 4.6 %collective-permute-start.45 = (f32[4,1,4,512]{3,2,1,0:T(4,128)S(1)}, f32[4,1,4,512]{3,2,1,0:T(4,128)S(1)}, u32[]{:S(2)}, u32[]{:S(2)}) collective-permute-start(f32[4,1,4,512]{3,2,1,0:T(4,128)S(1)} %get-tuple-element.121), channel_id=1, source_target_pairs={{1,0},{2,1},{3,2},{4,3},{5,4},{6,5},{7,6},{8,7},{9,8},{10,9},{11,1... | collective-permute-start | bytes 98312 | tf_op jit(solution)/shard_map/ppermute | solution.py:26
  343.2 4.6 %collective-permute-start.47 = (f32[4,1,4,512]{3,2,1,0:T(4,128)S(1)}, f32[4,1,4,512]{3,2,1,0:T(4,128)S(1)}, u32[]{:S(2)}, u32[]{:S(2)}) collective-permute-start(f32[4,1,4,512]{3,2,1,0:T(4,128)S(1)} %get-tuple-element.115), channel_id=1, source_target_pairs={{1,0},{2,1},{3,2},{4,3},{5,4},{6,5},{7,6},{8,7},{9,8},{10,9},{11,1... | collective-permute-start | bytes 98312 | tf_op jit(solution)/shard_map/ppermute | solution.py:26
  352.6 6.7 %broadcast_in_dim.50 = f32[4,4,8,512,2]{2,4,3,1,0:T(2,128)} broadcast(f32[4,4,8,512]{2,3,1,0:T(8,128)} %copy.406), dimensions={0,1,2,3} | broadcast | bytes 786432 | tf_op jit(solution)/shard_map/broadcast_in_dim | solution.py:94
  359.3 5.1 %copy.407 = f32[4,4,8,1024]{3,2,1,0:T(8,128)S(1)} copy(f32[4,4,8,1024]{2,3,1,0:T(8,128)} %bitcast.110) | data formatting | bytes 1048576 | tf_op jit(solution)/shard_map/reshape | solution.py:94
  364.8 4.5 %collective-permute-start.49 = (f32[4,1,8,1024]{3,2,1,0:T(8,128)S(1)}, f32[4,1,8,1024]{3,2,1,0:T(8,128)S(1)}, u32[]{:S(2)}, u32[]{:S(2)}) collective-permute-start(f32[4,1,8,1024]{3,2,1,0:T(8,128)S(1)} %get-tuple-element.35), channel_id=1, source_target_pairs={{1,0},{2,1},{3,2},{4,3},{5,4},{6,5},{7,6},{8,7},{9,8},{10,9},{11,1... | collective-permute-start | bytes 393224 | tf_op jit(solution)/shard_map/ppermute | solution.py:26
  372.8 4.5 %collective-permute-start.51 = (f32[4,1,8,1024]{3,2,1,0:T(8,128)S(1)}, f32[4,1,8,1024]{3,2,1,0:T(8,128)S(1)}, u32[]{:S(2)}, u32[]{:S(2)}) collective-permute-start(f32[4,1,8,1024]{3,2,1,0:T(8,128)S(1)} %get-tuple-element.25), channel_id=1, source_target_pairs={{1,0},{2,1},{3,2},{4,3},{5,4},{6,5},{7,6},{8,7},{9,8},{10,9},{11,1... | collective-permute-start | bytes 393224 | tf_op jit(solution)/shard_map/ppermute | solution.py:26
  389.5 4.6 %collective-permute-done.53 = f32[8,1,8,1024]{3,2,1,0:T(8,128)S(1)} collective-permute-done((f32[8,1,8,1024]{3,2,1,0:T(8,128)S(1)}, f32[8,1,8,1024]{3,2,1,0:T(8,128)S(1)}, u32[]{:S(2)}, u32[]{:S(2)}) %collective-permute-start.53) | collective-permute-done | bytes 262176 | tf_op jit(solution)/shard_map/ppermute | solution.py:23
  (364 shorter events, 153.2 us)
Async XLA Ops:
  0.6 62.8 %collective-permute-start.12 = (f32[1,2,256]{2,1,0:T(2,128)}, f32[1,2,256]{2,1,0:T(2,128)S(1)}, u32[]{:S(2)}, u32[]{:S(2)}) collective-permute-start(f32[1,2,256]{2,1,0:T(2,128)} %param.9), channel_id=1, source_target_pairs={{0,1},{1,2},{2,3},{3,4},{4,5},{5,6},{6,7},{7,8},{8,9},{9,10},{10,1... | collective-permute-start | bytes 6152 | tf_op jit(solution)/shard_map/ppermute | solution.py:23
  1.1 66.8 %collective-permute-start.13 = (f32[1,2,256]{2,1,0:T(2,128)}, f32[1,2,256]{2,1,0:T(2,128)S(1)}, u32[]{:S(2)}, u32[]{:S(2)}) collective-permute-start(f32[1,2,256]{2,1,0:T(2,128)} %param.9), channel_id=1, source_target_pairs={{1,0},{2,1},{3,2},{4,3},{5,4},{6,5},{7,6},{8,7},{9,8},{10,9},{11,1... | collective-permute-start | bytes 6152 | tf_op jit(solution)/shard_map/ppermute | solution.py:26
  7.0 62.5 %collective-permute-start = (f32[1,8,1024]{2,1,0:T(8,128)S(1)}, f32[1,8,1024]{2,1,0:T(8,128)S(1)}, u32[]{:S(2)}, u32[]{:S(2)}) collective-permute-start(f32[1,8,1024]{2,1,0:T(8,128)S(1)} %get-tuple-element.109), channel_id=1, source_target_pairs={{0,1},{1,2},{2,3},{3,4},{4,5},{5,6},{6,7},{7,8},{8,9},{9,10},{10,1... | collective-permute-start | bytes 98312 | tf_op jit(solution)/shard_map/ppermute | solution.py:23
  7.0 62.5 %collective-permute-start.1 = (f32[1,8,1024]{2,1,0:T(8,128)S(1)}, f32[1,8,1024]{2,1,0:T(8,128)S(1)}, u32[]{:S(2)}, u32[]{:S(2)}) collective-permute-start(f32[1,8,1024]{2,1,0:T(8,128)S(1)} %get-tuple-element.108), channel_id=1, source_target_pairs={{1,0},{2,1},{3,2},{4,3},{5,4},{6,5},{7,6},{8,7},{9,8},{10,9},{11,1... | collective-permute-start | bytes 98312 | tf_op jit(solution)/shard_map/ppermute | solution.py:26
  12.1 57.0 %collective-permute-start.6 = (f32[1,4,512]{2,1,0:T(4,128)S(1)}, f32[1,4,512]{2,1,0:T(4,128)S(1)}, u32[]{:S(2)}, u32[]{:S(2)}) collective-permute-start(f32[1,4,512]{2,1,0:T(4,128)S(1)} %get-tuple-element.165), channel_id=1, source_target_pairs={{0,1},{1,2},{2,3},{3,4},{4,5},{5,6},{6,7},{7,8},{8,9},{9,10},{10,1... | collective-permute-start | bytes 24584 | tf_op jit(solution)/shard_map/ppermute | solution.py:23
  70.0 7.2 %collective-permute-start.2 = (f32[4,1,8,1024]{3,2,1,0:T(8,128)S(1)}, f32[4,1,8,1024]{3,2,1,0:T(8,128)S(1)}, u32[]{:S(2)}, u32[]{:S(2)}) collective-permute-start(f32[4,1,8,1024]{3,2,1,0:T(8,128)S(1)} %get-tuple-element.76), channel_id=1, source_target_pairs={{0,1},{1,2},{2,3},{3,4},{4,5},{5,6},{6,7},{7,8},{8,9},{9,10},{10,1... | collective-permute-start | bytes 393224 | tf_op jit(solution)/shard_map/ppermute | solution.py:23
  138.2 8.7 %collective-permute-start.14 = (f32[4,1,2,256]{0,3,2,1:T(8,128)S(1)}, f32[4,1,2,256]{0,3,2,1:T(8,128)S(1)}, u32[]{:S(2)}, u32[]{:S(2)}) collective-permute-start(f32[4,1,2,256]{0,3,2,1:T(8,128)S(1)} %broadcast_multiply_fusion.2), channel_id=1, source_target_pairs={{0,1},{1,2},{2,3},{3,4},{4,5},{5,6},{6,7},{7,8},{8,9},{9,10},{10,1... | collective-permute-start | bytes 24584 | tf_op jit(solution)/shard_map/ppermute | solution.py:23
  138.3 8.6 %collective-permute-start.15 = (f32[4,1,2,256]{0,3,2,1:T(8,128)S(1)}, f32[4,1,2,256]{0,3,2,1:T(8,128)S(1)}, u32[]{:S(2)}, u32[]{:S(2)}) collective-permute-start(f32[4,1,2,256]{0,3,2,1:T(8,128)S(1)} %broadcast_multiply_fusion.2), channel_id=1, source_target_pairs={{1,0},{2,1},{3,2},{4,3},{5,4},{6,5},{7,6},{8,7},{9,8},{10,9},{11,1... | collective-permute-start | bytes 24584 | tf_op jit(solution)/shard_map/ppermute | solution.py:26
  148.4 8.7 %collective-permute-start.16 = (f32[4,1,2,256]{0,3,2,1:T(8,128)S(1)}, f32[4,1,2,256]{0,3,2,1:T(8,128)S(1)}, u32[]{:S(2)}, u32[]{:S(2)}) collective-permute-start(f32[4,1,2,256]{0,3,2,1:T(8,128)S(1)} %fusion.108), channel_id=1, source_target_pairs={{0,1},{1,2},{2,3},{3,4},{4,5},{5,6},{6,7},{7,8},{8,9},{9,10},{10,1... | collective-permute-start | bytes 24584 | tf_op jit(solution)/shard_map/ppermute | solution.py:23
  148.4 8.6 %collective-permute-start.17 = (f32[4,1,2,256]{0,3,2,1:T(8,128)S(1)}, f32[4,1,2,256]{0,3,2,1:T(8,128)S(1)}, u32[]{:S(2)}, u32[]{:S(2)}) collective-permute-start(f32[4,1,2,256]{0,3,2,1:T(8,128)S(1)} %fusion.108), channel_id=1, source_target_pairs={{1,0},{2,1},{3,2},{4,3},{5,4},{6,5},{7,6},{8,7},{9,8},{10,9},{11,1... | collective-permute-start | bytes 24584 | tf_op jit(solution)/shard_map/ppermute | solution.py:26
  157.7 8.6 %collective-permute-start.18 = (f32[4,1,2,256]{0,3,2,1:T(8,128)S(1)}, f32[4,1,2,256]{0,3,2,1:T(8,128)S(1)}, u32[]{:S(2)}, u32[]{:S(2)}) collective-permute-start(f32[4,1,2,256]{0,3,2,1:T(8,128)S(1)} %fusion.111), channel_id=1, source_target_pairs={{0,1},{1,2},{2,3},{3,4},{4,5},{5,6},{6,7},{7,8},{8,9},{9,10},{10,1... | collective-permute-start | bytes 24584 | tf_op jit(solution)/shard_map/ppermute | solution.py:23
  157.8 8.5 %collective-permute-start.19 = (f32[4,1,2,256]{0,3,2,1:T(8,128)S(1)}, f32[4,1,2,256]{0,3,2,1:T(8,128)S(1)}, u32[]{:S(2)}, u32[]{:S(2)}) collective-permute-start(f32[4,1,2,256]{0,3,2,1:T(8,128)S(1)} %fusion.111), channel_id=1, source_target_pairs={{1,0},{2,1},{3,2},{4,3},{5,4},{6,5},{7,6},{8,7},{9,8},{10,9},{11,1... | collective-permute-start | bytes 24584 | tf_op jit(solution)/shard_map/ppermute | solution.py:26
  200.3 7.3 %collective-permute-start.24 = (f32[4,1,8,1024]{3,2,1,0:T(8,128)S(1)}, f32[4,1,8,1024]{3,2,1,0:T(8,128)S(1)}, u32[]{:S(2)}, u32[]{:S(2)}) collective-permute-start(f32[4,1,8,1024]{3,2,1,0:T(8,128)S(1)} %get-tuple-element.64), channel_id=1, source_target_pairs={{0,1},{1,2},{2,3},{3,4},{4,5},{5,6},{6,7},{7,8},{8,9},{9,10},{10,1... | collective-permute-start | bytes 393224 | tf_op jit(solution)/shard_map/ppermute | solution.py:23
  200.4 7.2 %collective-permute-start.25 = (f32[4,1,8,1024]{3,2,1,0:T(8,128)S(1)}, f32[4,1,8,1024]{3,2,1,0:T(8,128)S(1)}, u32[]{:S(2)}, u32[]{:S(2)}) collective-permute-start(f32[4,1,8,1024]{3,2,1,0:T(8,128)S(1)} %get-tuple-element.65), channel_id=1, source_target_pairs={{1,0},{2,1},{3,2},{4,3},{5,4},{6,5},{7,6},{8,7},{9,8},{10,9},{11,1... | collective-permute-start | bytes 393224 | tf_op jit(solution)/shard_map/ppermute | solution.py:26
  208.4 7.3 %collective-permute-start.26 = (f32[4,1,8,1024]{3,2,1,0:T(8,128)S(1)}, f32[4,1,8,1024]{3,2,1,0:T(8,128)S(1)}, u32[]{:S(2)}, u32[]{:S(2)}) collective-permute-start(f32[4,1,8,1024]{3,2,1,0:T(8,128)S(1)} %get-tuple-element.58), channel_id=1, source_target_pairs={{0,1},{1,2},{2,3},{3,4},{4,5},{5,6},{6,7},{7,8},{8,9},{9,10},{10,1... | collective-permute-start | bytes 393224 | tf_op jit(solution)/shard_map/ppermute | solution.py:23
  208.4 7.2 %collective-permute-start.27 = (f32[4,1,8,1024]{3,2,1,0:T(8,128)S(1)}, f32[4,1,8,1024]{3,2,1,0:T(8,128)S(1)}, u32[]{:S(2)}, u32[]{:S(2)}) collective-permute-start(f32[4,1,8,1024]{3,2,1,0:T(8,128)S(1)} %get-tuple-element.59), channel_id=1, source_target_pairs={{1,0},{2,1},{3,2},{4,3},{5,4},{6,5},{7,6},{8,7},{9,8},{10,9},{11,1... | collective-permute-start | bytes 393224 | tf_op jit(solution)/shard_map/ppermute | solution.py:26
  216.5 7.3 %collective-permute-start.28 = (f32[4,1,8,1024]{3,2,1,0:T(8,128)S(1)}, f32[4,1,8,1024]{3,2,1,0:T(8,128)S(1)}, u32[]{:S(2)}, u32[]{:S(2)}) collective-permute-start(f32[4,1,8,1024]{3,2,1,0:T(8,128)S(1)} %get-tuple-element.52), channel_id=1, source_target_pairs={{0,1},{1,2},{2,3},{3,4},{4,5},{5,6},{6,7},{7,8},{8,9},{9,10},{10,1... | collective-permute-start | bytes 393224 | tf_op jit(solution)/shard_map/ppermute | solution.py:23
  216.5 7.2 %collective-permute-start.29 = (f32[4,1,8,1024]{3,2,1,0:T(8,128)S(1)}, f32[4,1,8,1024]{3,2,1,0:T(8,128)S(1)}, u32[]{:S(2)}, u32[]{:S(2)}) collective-permute-start(f32[4,1,8,1024]{3,2,1,0:T(8,128)S(1)} %get-tuple-element.53), channel_id=1, source_target_pairs={{1,0},{2,1},{3,2},{4,3},{5,4},{6,5},{7,6},{8,7},{9,8},{10,9},{11,1... | collective-permute-start | bytes 393224 | tf_op jit(solution)/shard_map/ppermute | solution.py:26
  232.5 14.9 %collective-permute-start.32 = (f32[4,1,8,1024]{3,2,1,0:T(8,128)S(1)}, f32[4,1,8,1024]{3,2,1,0:T(8,128)S(1)}, u32[]{:S(2)}, u32[]{:S(2)}) collective-permute-start(f32[4,1,8,1024]{3,2,1,0:T(8,128)S(1)} %get-tuple-element.40), channel_id=1, source_target_pairs={{0,1},{1,2},{2,3},{3,4},{4,5},{5,6},{6,7},{7,8},{8,9},{9,10},{10,1... | collective-permute-start | bytes 393224 | tf_op jit(solution)/shard_map/ppermute | solution.py:23
  232.6 17.3 %collective-permute-start.33 = (f32[4,1,8,1024]{3,2,1,0:T(8,128)S(1)}, f32[4,1,8,1024]{3,2,1,0:T(8,128)S(1)}, u32[]{:S(2)}, u32[]{:S(2)}) collective-permute-start(f32[4,1,8,1024]{3,2,1,0:T(8,128)S(1)} %get-tuple-element.41), channel_id=1, source_target_pairs={{1,0},{2,1},{3,2},{4,3},{5,4},{6,5},{7,6},{8,7},{9,8},{10,9},{11,1... | collective-permute-start | bytes 393224 | tf_op jit(solution)/shard_map/ppermute | solution.py:26
  302.6 8.5 %collective-permute-start.38 = (f32[4,1,2,256]{0,3,2,1:T(8,128)S(1)}, f32[4,1,2,256]{0,3,2,1:T(8,128)S(1)}, u32[]{:S(2)}, u32[]{:S(2)}) collective-permute-start(f32[4,1,2,256]{0,3,2,1:T(8,128)S(1)} %broadcast_multiply_fusion.1), channel_id=1, source_target_pairs={{0,1},{1,2},{2,3},{3,4},{4,5},{5,6},{6,7},{7,8},{8,9},{9,10},{10,1... | collective-permute-start | bytes 24584 | tf_op jit(solution)/shard_map/ppermute | solution.py:23
  302.6 8.5 %collective-permute-start.39 = (f32[4,1,2,256]{0,3,2,1:T(8,128)S(1)}, f32[4,1,2,256]{0,3,2,1:T(8,128)S(1)}, u32[]{:S(2)}, u32[]{:S(2)}) collective-permute-start(f32[4,1,2,256]{0,3,2,1:T(8,128)S(1)} %broadcast_multiply_fusion.1), channel_id=1, source_target_pairs={{1,0},{2,1},{3,2},{4,3},{5,4},{6,5},{7,6},{8,7},{9,8},{10,9},{11,1... | collective-permute-start | bytes 24584 | tf_op jit(solution)/shard_map/ppermute | solution.py:26
  312.7 8.7 %collective-permute-start.40 = (f32[4,1,2,256]{0,3,2,1:T(8,128)S(1)}, f32[4,1,2,256]{0,3,2,1:T(8,128)S(1)}, u32[]{:S(2)}, u32[]{:S(2)}) collective-permute-start(f32[4,1,2,256]{0,3,2,1:T(8,128)S(1)} %fusion.98), channel_id=1, source_target_pairs={{0,1},{1,2},{2,3},{3,4},{4,5},{5,6},{6,7},{7,8},{8,9},{9,10},{10,1... | collective-permute-start | bytes 24584 | tf_op jit(solution)/shard_map/ppermute | solution.py:23
  312.7 8.7 %collective-permute-start.41 = (f32[4,1,2,256]{0,3,2,1:T(8,128)S(1)}, f32[4,1,2,256]{0,3,2,1:T(8,128)S(1)}, u32[]{:S(2)}, u32[]{:S(2)}) collective-permute-start(f32[4,1,2,256]{0,3,2,1:T(8,128)S(1)} %fusion.98), channel_id=1, source_target_pairs={{1,0},{2,1},{3,2},{4,3},{5,4},{6,5},{7,6},{8,7},{9,8},{10,9},{11,1... | collective-permute-start | bytes 24584 | tf_op jit(solution)/shard_map/ppermute | solution.py:26
  322.0 8.6 %collective-permute-start.42 = (f32[4,1,2,256]{0,3,2,1:T(8,128)S(1)}, f32[4,1,2,256]{0,3,2,1:T(8,128)S(1)}, u32[]{:S(2)}, u32[]{:S(2)}) collective-permute-start(f32[4,1,2,256]{0,3,2,1:T(8,128)S(1)} %fusion.101), channel_id=1, source_target_pairs={{0,1},{1,2},{2,3},{3,4},{4,5},{5,6},{6,7},{7,8},{8,9},{9,10},{10,1... | collective-permute-start | bytes 24584 | tf_op jit(solution)/shard_map/ppermute | solution.py:23
  322.1 8.5 %collective-permute-start.43 = (f32[4,1,2,256]{0,3,2,1:T(8,128)S(1)}, f32[4,1,2,256]{0,3,2,1:T(8,128)S(1)}, u32[]{:S(2)}, u32[]{:S(2)}) collective-permute-start(f32[4,1,2,256]{0,3,2,1:T(8,128)S(1)} %fusion.101), channel_id=1, source_target_pairs={{1,0},{2,1},{3,2},{4,3},{5,4},{6,5},{7,6},{8,7},{9,8},{10,9},{11,1... | collective-permute-start | bytes 24584 | tf_op jit(solution)/shard_map/ppermute | solution.py:26
  364.7 7.3 %collective-permute-start.48 = (f32[4,1,8,1024]{3,2,1,0:T(8,128)S(1)}, f32[4,1,8,1024]{3,2,1,0:T(8,128)S(1)}, u32[]{:S(2)}, u32[]{:S(2)}) collective-permute-start(f32[4,1,8,1024]{3,2,1,0:T(8,128)S(1)} %get-tuple-element.34), channel_id=1, source_target_pairs={{0,1},{1,2},{2,3},{3,4},{4,5},{5,6},{6,7},{7,8},{8,9},{9,10},{10,1... | collective-permute-start | bytes 393224 | tf_op jit(solution)/shard_map/ppermute | solution.py:23
  364.8 7.2 %collective-permute-start.49 = (f32[4,1,8,1024]{3,2,1,0:T(8,128)S(1)}, f32[4,1,8,1024]{3,2,1,0:T(8,128)S(1)}, u32[]{:S(2)}, u32[]{:S(2)}) collective-permute-start(f32[4,1,8,1024]{3,2,1,0:T(8,128)S(1)} %get-tuple-element.35), channel_id=1, source_target_pairs={{1,0},{2,1},{3,2},{4,3},{5,4},{6,5},{7,6},{8,7},{9,8},{10,9},{11,1... | collective-permute-start | bytes 393224 | tf_op jit(solution)/shard_map/ppermute | solution.py:26
  372.8 7.3 %collective-permute-start.50 = (f32[4,1,8,1024]{3,2,1,0:T(8,128)S(1)}, f32[4,1,8,1024]{3,2,1,0:T(8,128)S(1)}, u32[]{:S(2)}, u32[]{:S(2)}) collective-permute-start(f32[4,1,8,1024]{3,2,1,0:T(8,128)S(1)} %get-tuple-element.24), channel_id=1, source_target_pairs={{0,1},{1,2},{2,3},{3,4},{4,5},{5,6},{6,7},{7,8},{8,9},{9,10},{10,1... | collective-permute-start | bytes 393224 | tf_op jit(solution)/shard_map/ppermute | solution.py:23
  372.8 7.2 %collective-permute-start.51 = (f32[4,1,8,1024]{3,2,1,0:T(8,128)S(1)}, f32[4,1,8,1024]{3,2,1,0:T(8,128)S(1)}, u32[]{:S(2)}, u32[]{:S(2)}) collective-permute-start(f32[4,1,8,1024]{3,2,1,0:T(8,128)S(1)} %get-tuple-element.25), channel_id=1, source_target_pairs={{1,0},{2,1},{3,2},{4,3},{5,4},{6,5},{7,6},{8,7},{9,8},{10,9},{11,1... | collective-permute-start | bytes 393224 | tf_op jit(solution)/shard_map/ppermute | solution.py:26
  381.1 8.3 %collective-permute-start.52 = (f32[8,1,8,1024]{3,2,1,0:T(8,128)S(1)}, f32[8,1,8,1024]{3,2,1,0:T(8,128)S(1)}, u32[]{:S(2)}, u32[]{:S(2)}) collective-permute-start(f32[8,1,8,1024]{3,2,1,0:T(8,128)S(1)} %get-tuple-element.20), channel_id=1, source_target_pairs={{1,0},{2,1},{3,2},{4,3},{5,4},{6,5},{7,6},{8,7},{9,8},{10,9},{11,1... | collective-permute-start | bytes 786440 | tf_op jit(solution)/shard_map/ppermute | solution.py:26
  385.6 8.5 %collective-permute-start.53 = (f32[8,1,8,1024]{3,2,1,0:T(8,128)S(1)}, f32[8,1,8,1024]{3,2,1,0:T(8,128)S(1)}, u32[]{:S(2)}, u32[]{:S(2)}) collective-permute-start(f32[8,1,8,1024]{3,2,1,0:T(8,128)S(1)} %get-tuple-element.21), channel_id=1, source_target_pairs={{0,1},{1,2},{2,3},{3,4},{4,5},{5,6},{6,7},{7,8},{8,9},{9,10},{10,1... | collective-permute-start | bytes 786440 | tf_op jit(solution)/shard_map/ppermute | solution.py:23
  (77 other events, 1452.5 us)
where the time goes:
time: 401 us; the launch traced here: 396 us
  starting transfers between devices  135 us (34%)
  other arithmetic  110 us (27%)
  local copies, waits for them, and re-layouts  80.8 us (20%)
  waiting for transfers between devices  67.8 us (17%)
    ppermute x27, starting transfers between devices, padded_2(): lax.ppermute(lax.slice_in_dim(block, 0, width, axis=dim), axis, backward)  133 us
    ppermute x27, waiting for transfers between devices, padded_2(): lax.ppermute(lax.slice_in_dim(block, block.shape[dim] - width, None, axis...  61 us
    reduce_sum x6, other arithmetic, restrict(): return grouped.sum(axis=(2, 4, 6))  53.6 us
    scatter-add x1, other arithmetic, local(): source = jnp.zeros((sources, cells_dev), jnp.float32).at[:, receiver_cell...  29.5 us
    broadcast_in_dim x6, local copies, waits for them, and re-layouts, prolong(): jnp.repeat(jnp.repeat(jnp.repeat(field, 2, axis=1), 2, axis=2), 2, axis=3)  18 us
    sub x2, local copies, waits for them, and re-layouts, vcycle(): right_mid = restrict(right - image)  17.4 us
    add x18, other arithmetic, sweep(): return padded[:, 1:-1] + OMEGA * ((right - image) / own_diag)  11.2 us
    reshape x2, local copies, waits for them, and re-layouts, prolong(): jnp.repeat(jnp.repeat(jnp.repeat(field, 2, axis=1), 2, axis=2), 2, axis=3)  10.2 us
  transfers between devices with their start and end apart: 54, of which 32 were waited for; matrix products, arithmetic and copies ran while one was open for 14% of the time, Pallas kernels for 0%

commit v1 on v0

v1 whole, which is shorter than its diff:
```python
import functools
import math

import jax
import jax.numpy as jnp
from jax import lax
from jax.experimental import pallas as pl
from jax.experimental.pallas import tpu as pltpu
from jax.sharding import PartitionSpec as P

OMEGA = 0.7
BETA = 0.05
LANES = 128
F32 = jnp.float32
BF16 = jnp.bfloat16
MESH = pl.DeviceIdType.MESH
NT = (((1,), (1,)), ((), ()))


def pieces(x, count):
    out = []
    for _ in range(count):
        part = x.astype(BF16)
        out.append(part)
        x = x - part.astype(F32)
    return out


def scatter_kernel(cells_ref, weights_ref, out_ref):
    azim, sources, depth_j, depth, _ = out_ref.shape
    radial = depth_j * LANES
    half = depth_j // 2
    rows = azim * half * depth
    count = cells_ref.shape[1]
    cell = cells_ref[...]
    a = cell // (depth * radial)
    z = (cell // radial) % depth
    i = cell % radial
    lane = i // depth_j
    j = i % depth_j
    high = (a * half + j // 2) * depth + z
    low = (j % 2) * LANES + lane
    chunk = 1024
    totals = [jnp.zeros((rows, 2 * LANES), F32) for _ in range(sources)]
    for start in range(0, count, chunk):
        at = slice(start, start + chunk)
        hot_low = jnp.where(
            lax.broadcasted_iota(jnp.int32, (2 * LANES, chunk), 0) == low[:, at], 1.0, 0.0
        ).astype(BF16)
        hit = lax.broadcasted_iota(jnp.int32, (rows, chunk), 0) == high[:, at]
        for s in range(sources):
            for part in pieces(weights_ref[s, :, at], 2):
                left = jnp.where(hit, part.astype(F32), 0.0).astype(BF16)
                totals[s] = totals[s] + lax.dot_general(
                    left, hot_low, NT, preferred_element_type=F32
                )
    for s in range(sources):
        grid = totals[s].reshape(azim, half, depth, 2 * LANES)
        for jh in range(half):
            for jl in range(2):
                out_ref[:, s, 2 * jh + jl] = grid[:, jh, :, jl * LANES:(jl + 1) * LANES]


def roll(x, shift, axis):
    return pltpu.roll(x, shift % x.shape[axis], axis)


def outward(v):
    return jnp.concatenate([v[1:], roll(v[:1], -1, 2)], axis=0)


def inward(v):
    return jnp.concatenate([roll(v[-1:], 1, 2), v[:-1]], axis=0)


def sublane(shape):
    return lax.broadcasted_iota(jnp.int32, shape, len(shape) - 2)


def order(size):
    j = size // LANES
    row = lax.broadcasted_iota(jnp.int32, (size, size), 0)
    col = lax.broadcasted_iota(jnp.int32, (size, size), 1)
    return jnp.where(row == (col % LANES) * j + col // LANES, 1.0, 0.0).astype(BF16)


def reorder(rows, matrix, dims):
    total = None
    for part in pieces(rows, 3):
        term = lax.dot_general(part, matrix, dims, preferred_element_type=F32)
        total = term if total is None else total + term
    return total


def radius(j, inner, spacing):
    shape = (j, 8, LANES)
    index = lax.broadcasted_iota(jnp.int32, shape, 2) * j + lax.broadcasted_iota(jnp.int32, shape, 0)
    index = index.astype(F32)
    return inner + spacing * (index + 0.5), inner + spacing * (index + 1.0), index


def arrange(raw_ref, out_ref, matrix, first, last):
    depth, size = raw_ref.shape[1:]
    cells = last - first
    if depth == 8:
        full = raw_ref[first:last]
    else:
        each = 8 // depth
        at = sublane((cells, 8, size)) // each
        full = jnp.broadcast_to(raw_ref[first:last, 0:1, :], (cells, 8, size))
        for z in range(1, depth):
            full = jnp.where(at == z, jnp.broadcast_to(raw_ref[first:last, z:z + 1, :], (cells, 8, size)), full)
    out = reorder(full.reshape(cells * 8, size), matrix, (((1,), (0,)), ((), ())))
    for j in range(size // LANES):
        out_ref[first:last, j] = out[:, j * LANES:(j + 1) * LANES].reshape(cells, 8, LANES)


class Level:
    def __init__(self, refs, shift, spacing, inner, theta):
        self.sigma, self.face, self.radial, self.deep, self.diag, self.scale = refs
        self.shift = shift
        self.spacing = spacing
        self.inner = inner
        self.theta = theta
        self.count, self.j = self.sigma.shape[:2]

    def coefficients(self):
        h, theta, k, j = self.spacing, self.theta, self.shift, self.j
        centre, outer, index = radius(j, self.inner, h)
        to_radial = jnp.where(index < j * LANES - 1, outer * (theta * 0.5), 0.0)
        to_deep = jnp.where(sublane(centre.shape) < 8 - k, centre * (theta * 0.5), 0.0)
        to_face = (0.5 * h * h / theta) / centre
        to_own = (BETA * h * h * theta) * centre

        def faces(c, carry):
            self.face[c] = to_face * (self.sigma[c - 1] + self.sigma[c])
            return carry

        lax.fori_loop(1, self.count, faces, 0)

        def cell(c, carry):
            own = self.sigma[c]
            radial = to_radial * (own + outward(own))
            deep = to_deep * (own + roll(own, -k, 1))
            diag = (radial + inward(radial) + deep + roll(deep, k, 1)
                    + self.face[c] + self.face[c + 1] + to_own * own)
            self.radial[c] = radial
            self.deep[c] = deep
            self.diag[c] = diag
            self.scale[c] = OMEGA / diag
            return carry

        lax.fori_loop(1, self.count - 1, cell, 0)

    def near(self, field, c, g):
        v = field[c, g]
        radial, deep, k = self.radial[c], self.deep[c], self.shift
        return v, (self.face[c] * field[c - 1, g] + self.face[c + 1] * field[c + 1, g]
                   + radial * outward(v) + inward(radial * v)
                   + deep * roll(v, -k, 1) + roll(deep * v, k, 1))

    def first(self, right, out, lo, hi):
        def body(c, carry):
            scale = self.scale[c]
            for g in range(right.shape[1]):
                out[c, g] = scale * right[c, g]
            return carry

        lax.fori_loop(lo, hi, body, 0)

    def sweep(self, field, out, right, lo, hi):
        def body(c, carry):
            for g in range(right.shape[1]):
                v, near = self.near(field, c, g)
                out[c, g] = (1.0 - OMEGA) * v + self.scale[c] * (right[c, g] + near)
            return carry

        lax.fori_loop(lo, hi, body, 0)

    def residual(self, field, right, c, g):
        v, near = self.near(field, c, g)
        return right[c, g] - self.diag[c] * v + near


def pair_sum(x, k):
    lower = (sublane(x.shape) // k) % 2 == 0
    return x + jnp.where(lower, roll(x, -k, x.ndim - 2), roll(x, k, x.ndim - 2))


def halve(x):
    return x.reshape((x.shape[0] // 2, 2) + x.shape[1:]).sum(axis=1)


def twice(x):
    shape = x.shape
    wide = jnp.broadcast_to(x[:, None], (shape[0], 2) + shape[1:])
    return wide.reshape((2 * shape[0],) + shape[1:])


def spread(x, k, which):
    odd = (sublane(x.shape) // k) % 2 == 1
    if which == 0:
        return twice(jnp.where(odd, roll(x, k, 1), x))
    return twice(jnp.where(odd, x, roll(x, -k, 1)))


def restrict(level, field, right, out, first, target, cells, k):
    for m in range(cells):
        for q in range(right.shape[1] // 2):
            sums = []
            for g in (2 * q, 2 * q + 1):
                both = (level.residual(field, right, first + 2 * m, g)
                        + level.residual(field, right, first + 2 * m + 1, g))
                sums.append(pair_sum(halve(both), k))
            odd = (sublane(sums[0].shape) // k) % 2 == 1
            out[target + m, q] = jnp.where(odd, sums[1], sums[0])


def prolong(field, coarse, out, lo, hi, offset, k):
    def body(c, carry):
        for q in range(coarse.shape[1]):
            x = coarse[c // 2 + offset, q]
            for which in range(2):
                g = 2 * q + which
                out[c, g] = field[c, g] + spread(x, k, which)
        return carry

    lax.fori_loop(lo, hi, body, 0)


def kernel(ring, inner, theta, forward_ref, sig0_ref, sig1_ref, sig2_ref, b_ref, adj_ref, grad_ref,
           raw0, raw1, raw2, uedge, *rest):
    rest = list(rest)
    refs = [[rest.pop(0) for _ in range(6)] for _ in range(3)]
    B, VA, VB, VC, VD = [rest.pop(0) for _ in range(5)]
    MA, MD, CA, CB = [rest.pop(0) for _ in range(4)]
    cyc = [[rest.pop(0) for _ in range(4)] for _ in range(2)]
    wide, send_sems, recv_sems = rest
    sources = forward_ref.shape[0]
    size = forward_ref.shape[-1]
    me = lax.axis_index("azim")
    inv = lax.axis_index("inv")
    used = []

    def device(offset):
        return (inv, lax.rem(me + offset + ring, ring))

    def send(src, dst, offset):
        n = len(used)
        copy = pltpu.make_async_remote_copy(
            src_ref=src, dst_ref=dst, send_sem=send_sems.at[n], recv_sem=recv_sems.at[n],
            device_id=device(offset), device_id_type=MESH)
        copy.start()
        used.append(copy)
        return copy

    def arrived(copies):
        for copy in copies:
            copy.wait_recv()

    barrier = pltpu.get_barrier_semaphore()
    offsets = [s * k for k in range(1, 6) for s in (1, -1)]
    for offset in offsets:
        pl.semaphore_signal(barrier, inc=1, device_id=device(offset), device_id_type=MESH)
    pl.semaphore_wait(barrier, len(offsets))

    got_sigma = [
        send(sig0_ref, raw0.at[0:4], 1), send(sig0_ref, raw0.at[8:12], -1),
        send(sig1_ref, raw1.at[2:4], 1), send(sig1_ref, raw1.at[6:8], -1),
        send(sig1_ref, raw1.at[0:2], 2), send(sig1_ref, raw1.at[8:10], -2),
    ]
    for k in range(1, 6):
        got_sigma.append(send(sig2_ref, raw2.at[5 - k:6 - k], k))
        got_sigma.append(send(sig2_ref, raw2.at[5 + k:6 + k], -k))
    got_b = [send(b_ref.at[2:4], B.at[2:4], 1), send(b_ref.at[0:2], B.at[8:10], -1)]
    got_b_far = [send(b_ref.at[1:2], B.at[1:2], 1), send(b_ref.at[2:3], B.at[10:11], -1)]
    got_u = [send(forward_ref.at[:, 3:4], uedge.at[0], 1), send(forward_ref.at[:, 0:1], uedge.at[1], -1)]

    raw0[4:8] = sig0_ref[...]
    raw1[4:6] = sig1_ref[...]
    raw2[5:6] = sig2_ref[...]
    B[4:8] = b_ref[...]
    wide[...] = order(size)
    mid_order = order(size // 2)
    coarse_order = order(size // 4)

    fine = Level(refs[0], 1, 1, inner, theta)
    mid = Level(refs[1], 2, 2, inner, 2 * theta)
    coarse = Level(refs[2], 4, 4, inner, 4 * theta)
    arrived(got_sigma)
    arrange(raw0, fine.sigma, wide[...], 0, 12)
    fine.coefficients()
    arrange(raw1, mid.sigma, mid_order, 0, 10)
    mid.coefficients()
    arrange(raw2, coarse.sigma, coarse_order, 0, 11)
    coarse.coefficients()

    def correction(field, buffers):
        B1, MB, B2, ME = buffers
        restrict(fine, field, B, B1, 4, 4, 2, 1)
        got = [send(B1.at[4:6], B1.at[2:4], 1), send(B1.at[4:6], B1.at[6:8], -1)]
        if field is VB:
            got_far = [send(VB.at[4:7], VB.at[0:3], 1), send(VB.at[5:8], VB.at[9:12], -1)]
        else:
            got_far = [send(VD.at[5:7], VD.at[1:3], 1), send(VD.at[5:7], VD.at[9:11], -1)]
        arrived(got)
        mid.first(B1, MA, 2, 8)
        mid.sweep(MA, MB, B1, 3, 7)
        restrict(mid, MB, B1, B2, 4, 5, 1, 2)
        got = []
        for k in range(1, 5):
            got.append(send(B2.at[5:6], B2.at[5 - k:6 - k], k))
            got.append(send(B2.at[5:6], B2.at[5 + k:6 + k], -k))
        got_mid = [send(MB.at[4:5], MB.at[2:3], 1), send(MB.at[5:6], MB.at[7:8], -1)]
        arrived(got)
        coarse.first(B2, CA, 1, 10)
        coarse.sweep(CA, CB, B2, 2, 9)
        coarse.sweep(CB, CA, B2, 3, 8)
        coarse.sweep(CA, CB, B2, 4, 7)
        arrived(got_mid)
        prolong(MB, CB, MA, 2, 8, 3, 2)
        mid.sweep(MA, MD, B1, 3, 7)
        mid.sweep(MD, ME, B1, 4, 6)
        got = [send(ME.at[4:6], ME.at[2:4], 1), send(ME.at[4:6], ME.at[6:8], -1)]
        arrived(got_far)
        arrived(got)
        return ME

    arrived(got_b)
    fine.first(B, VA, 2, 10)
    fine.sweep(VA, VB, B, 3, 9)
    fix = correction(VB, cyc[0])
    arrived(got_b_far)
    prolong(VB, fix, VA, 0, 12, 2, 1)
    fine.sweep(VA, VC, B, 1, 11)
    fine.sweep(VC, VA, B, 2, 10)
    fine.sweep(VA, VC, B, 3, 9)
    fine.sweep(VC, VD, B, 4, 8)
    arrived([send(VD.at[7:8], VD.at[3:4], 1), send(VD.at[4:5], VD.at[8:9], -1)])
    fix = correction(VD, cyc[1])
    prolong(VD, fix, VA, 1, 11, 2, 1)
    fine.sweep(VA, VC, B, 2, 10)
    fine.sweep(VC, VA, B, 3, 9)

    def natural(lo, hi):
        cells = hi - lo
        rows = jnp.concatenate(
            [VA[lo:hi, :, j].reshape(cells * sources * 8, LANES) for j in range(size // LANES)], axis=1)
        return reorder(rows, wide[...], NT).reshape(cells, sources, 8, size)

    w = natural(3, 9)
    lane = lax.broadcasted_iota(jnp.int32, (8, size), 1)
    index = lane.astype(F32)
    centre = inner + (index + 0.5)
    outer = inner + (index + 1.0)
    to_radial = jnp.where(lane < size - 1, outer * (0.5 * theta), 0.0)
    to_deep = jnp.where(sublane((8, size)) < 7, centre * (0.5 * theta), 0.0)
    to_azim = (0.5 / theta) / centre
    to_own = (BETA * theta) * centre
    arrived(got_u)

    def forward_at(c, s):
        if c < 0:
            return uedge[0, s, 0]
        if c > 3:
            return uedge[1, s, 0]
        return forward_ref[s, c]

    face = None
    for c in range(-1, 4):
        total = None
        for s in range(sources):
            term = (forward_at(c + 1, s) - forward_at(c, s)) * (w[c + 2, s] - w[c + 1, s])
            total = term if total is None else total + term
        before, face = face, total
        if c < 0:
            continue
        radial = deep = own = None
        for s in range(sources):
            u, x = forward_at(c, s), w[c + 1, s]
            adj_ref[s, c] = x
            terms = ((roll(u, -1, 1) - u) * (roll(x, -1, 1) - x),
                     (roll(u, -1, 0) - u) * (roll(x, -1, 0) - x), u * x)
            if s == 0:
                radial, deep, own = terms
            else:
                radial, deep, own = radial + terms[0], deep + terms[1], own + terms[2]
        radial = radial * to_radial
        deep = deep * to_deep
        grad_ref[c] = -(to_azim * (before + face) + radial + roll(radial, 1, 1)
                        + deep + roll(deep, 1, 0) + to_own * own)

    for copy in used:
        copy.wait_send()


def local(forward_field, conductivity, conductivity_mid, conductivity_coarse, receiver_cells, receiver_weights):
    sources, azim, depth, size = forward_field.shape
    ring = lax.axis_size("azim")
    total_azim = azim * ring
    inner = total_azim // 6
    theta = 2.0 * math.pi / total_azim
    j = size // LANES
    vmem = pl.BlockSpec(memory_space=pltpu.VMEM)
    source = pl.pallas_call(
        scatter_kernel,
        out_shape=jax.ShapeDtypeStruct((azim, sources, j, depth, LANES), F32),
        in_specs=[vmem] * 2,
        out_specs=vmem,
        compiler_params=pltpu.CompilerParams(vmem_limit_bytes=48 * 1024 * 1024),
    )(receiver_cells, receiver_weights)

    def field(cells, groups, level_j):
        return pltpu.VMEM((cells, groups, level_j, 8, LANES), F32)

    def level(cells, level_j):
        return [pltpu.VMEM((cells, level_j, 8, LANES), F32)] * 6

    one_cycle = [field(10, 2, j // 2), field(10, 2, j // 2), field(11, 1, j // 4), field(10, 2, j // 2)]
    scratch = [
        pltpu.VMEM((12, depth, size), F32),
        pltpu.VMEM((10, depth // 2, size // 2), F32),
        pltpu.VMEM((11, depth // 4, size // 4), F32),
        pltpu.VMEM((2, sources, 1, depth, size), F32),
        *level(12, j), *level(10, j // 2), *level(11, j // 4),
        *[field(12, sources, j)] * 5,
        *[field(10, 2, j // 2)] * 2,
        *[field(11, 1, j // 4)] * 2,
        *one_cycle, *one_cycle,
        pltpu.VMEM((size, size), BF16),
        pltpu.SemaphoreType.DMA((64,)),
        pltpu.SemaphoreType.DMA((64,)),
    ]
    return pl.pallas_call(
        functools.partial(kernel, ring, inner, theta),
        out_shape=(
            jax.ShapeDtypeStruct((sources, azim, depth, size), F32),
            jax.ShapeDtypeStruct((azim, depth, size), F32),
        ),
        in_specs=[vmem] * 5,
        out_specs=(vmem, vmem),
        scratch_shapes=scratch,
        compiler_params=pltpu.CompilerParams(
            collective_id=0, has_side_effects=True, vmem_limit_bytes=48 * 1024 * 1024),
    )(forward_field, conductivity, conductivity_mid, conductivity_coarse, source)


def solution(mesh):
    placed = (
        P("inv", "azim", None, None),
        P("azim", "inv", None),
        P("azim", "inv", None),
        P("azim", "inv", None),
        P("azim", "inv"),
        P("inv", "azim", None),
    )
    return jax.shard_map(
        local,
        mesh=mesh,
        in_specs=placed,
        out_specs=(P("inv", "azim", None, None), P("azim", "inv", None)),
        check_vma=False,
    )
```

time: 401 us -> 80.7 us (0.20); the launches traced: 396 us -> 80.4 us
  starting transfers between devices: 135 us -> 0 us
  other arithmetic: 110 us -> 0 us
  local copies, waits for them, and re-layouts: 80.8 us -> 3.91 us
  Pallas kernels: 0 us -> 75.8 us
  waiting for transfers between devices: 67.8 us -> 0 us
    ppermute x54 -> x0, starting transfers between devices: 135 us -> none  [the longest x27 133 us: padded_2(): lax.ppermute(lax.slice_in_dim(block, 0, width, axis=dim), axis, backward)]
    pallas_call x0 -> x2, Pallas kernels: none -> 75.8 us  [the longest x1 70.4 us: local(): pl.pallas_call(functools.partial(kernel, ring, inner, theta), out_shape=(...]
    ppermute x54 -> x0, waiting for transfers between devices: 67.8 us -> none  [the longest x27 61 us: padded_2(): lax.ppermute(lax.slice_in_dim(block, block.shape[dim] - width, None, axis...]
    reduce_sum x10 -> x0, other arithmetic: 55.2 us -> none  [the longest x6 53.6 us: restrict(): return grouped.sum(axis=(2, 4, 6))]
    scatter-add x1 -> x0, other arithmetic: 29.5 us -> none  [local(): source = jnp.zeros((sources, cells_dev), jnp.float32).at[:, receiver_cell...]
    reshape x8 -> x0, local copies, waits for them, and re-layouts: 27.9 us -> none  [the longest x2 10.2 us: prolong(): jnp.repeat(jnp.repeat(jnp.repeat(field, 2, axis=1), 2, axis=2), 2, axis=3)]
    broadcast_in_dim x14 -> x0, local copies, waits for them, and re-layouts: 20.3 us -> none  [the longest x6 18 us: prolong(): jnp.repeat(jnp.repeat(jnp.repeat(field, 2, axis=1), 2, axis=2), 2, axis=3)]
    sub x2 -> x0, local copies, waits for them, and re-layouts: 17.4 us -> none  [vcycle(): right_mid = restrict(right - image)]
  transfers between devices with their start and end apart: 54 -> 0, of which waited for: 32 -> 0; matrix products, arithmetic and copies ran while one was open for 14% -> 0% of each run, Pallas kernels for 0% -> 0%
where the time goes in v1:
time: 80.7 us; the launch traced here: 80.4 us
  Pallas kernels  75.8 us (94%)
  local copies, waits for them, and re-layouts  3.91 us (5%)
    pallas_call x1, Pallas kernels, local(): pl.pallas_call(functools.partial(kernel, ring, inner, theta), out_shape=(...  70.4 us
    pallas_call x1, Pallas kernels, local(): pl.pallas_call(scatter_kernel, out_shape=jax.ShapeDtypeStruct((azim, sour...  5.47 us
    unnamed x14, local copies, waits for them, and re-layouts  3.91 us

profile of v1, /device:TPU:0, one launch (start us, length us, event | category | flops | bytes accessed | tf_op | source)
XLA Modules:
  0.0 80.4 jit_solution(1859912813175275733)
XLA Ops:
  0.6 0.0 copy-start.2
  0.6 0.8 %copy-done.2 = f32[4,1,4096]{2,1,0:T(1,128)S(1)} copy-done((f32[4,1,4096]{2,1,0:T(1,128)S(1)}, f32[4,1,4096]{2,1,0:T(1,128)}, u32[]{:S(2)}) %copy-start.2) | copy-done | bytes 65560
  1.5 0.0 copy-start.4
  1.5 0.7 copy-done.4
  2.2 0.0 copy-start
  2.2 0.0 copy-start.3
  2.2 0.0 copy-start.5
  2.2 5.5 %shard_map.77.b_ref = f32[4,4,8,8,128]{4,3,2,1,0:T(8,128)S(1)} custom-call(s32[1,4096]{1,0:T(1,128)S(1)} %copy-done.4, f32[4,1,4096]{2,1,0:T(1,128)S(1)} %copy-done.2), custom_call_target="tpu_custom_call" | custom-call | tf_op jit(solution)/shard_map/pallas_call | solution.py:405
  7.7 0.0 copy-done
  7.7 0.0 copy-done.3
  7.7 0.0 copy-done.5
  7.7 0.0 copy-start.1
  7.7 0.9 %copy-done.1 = f32[4,8,1024]{2,1,0:T(8,128)S(1)} copy-done((f32[4,8,1024]{2,1,0:T(8,128)S(1)}, f32[4,8,1024]{2,1,0:T(8,128)}, u32[]{:S(2)}) %copy-start.1) | copy-done | bytes 131096
  8.6 70.4 %shard_map.78 = (f32[4,4,8,1024]{3,2,1,0:T(8,128)S(1)}, f32[4,8,1024]{2,1,0:T(8,128)S(1)}) custom-call(f32[4,4,8,1024]{3,2,1,0:T(8,128)S(1)} %copy-done, f32[4,8,1024]{2,1,0:T(8,128)S(1)} %copy-done.1, f32[2,4,512]{2,1,0:T(4,128)S(1)} %copy-done.3, f32[1,2,256]{2,1,0:T(2,128)S(1)} %copy-done.5, f32[4,4,8,8,128]{4,3,2,1,0:T(8,128)S(1)} %shard_map.77.b_ref), custom_call_target="tpu_custom_call" | custom-call | tf_op jit(solution)/shard_map/pallas_call | solution.py:434
  79.0 0.8 copy.10
  79.8 0.7 copy.11
Async XLA Ops:
  0.6 0.8 %copy-start.2 = (f32[4,1,4096]{2,1,0:T(1,128)S(1)}, f32[4,1,4096]{2,1,0:T(1,128)}, u32[]{:S(2)}) copy-start(f32[4,1,4096]{2,1,0:T(1,128)} %weights_ref.1) | copy-start | bytes 196612
  1.5 0.7 copy-start.4
  2.2 5.5 %copy-start = (f32[4,4,8,1024]{3,2,1,0:T(8,128)S(1)}, f32[4,4,8,1024]{3,2,1,0:T(8,128)}, u32[]{:S(2)}) copy-start(f32[4,4,8,1024]{3,2,1,0:T(8,128)} %forward_ref.1) | copy-start | bytes 1572868
  2.2 5.5 %copy-start.3 = (f32[2,4,512]{2,1,0:T(4,128)S(1)}, f32[2,4,512]{2,1,0:T(4,128)}, u32[]{:S(2)}) copy-start(f32[2,4,512]{2,1,0:T(4,128)} %sig1_ref.1) | copy-start | bytes 49156
  2.2 5.5 %copy-start.5 = (f32[1,2,256]{2,1,0:T(2,128)S(1)}, f32[1,2,256]{2,1,0:T(2,128)}, u32[]{:S(2)}) copy-start(f32[1,2,256]{2,1,0:T(2,128)} %sig2_ref.1) | copy-start | bytes 6148
  7.7 0.9 %copy-start.1 = (f32[4,8,1024]{2,1,0:T(8,128)S(1)}, f32[4,8,1024]{2,1,0:T(8,128)}, u32[]{:S(2)}) copy-start(f32[4,8,1024]{2,1,0:T(8,128)} %sig0_ref.1) | copy-start | bytes 393220

commit v2 on v1

--- a/solution.py
+++ b/solution.py
@@ -26,36 +26,44 @@
     return out
 
 
-def scatter_kernel(cells_ref, weights_ref, out_ref):
+def log2(n):
+    assert n & (n - 1) == 0
+    return n.bit_length() - 1
+
+
+def scatter(cells_ref, weights_ref, out_ref):
     azim, sources, depth_j, depth, _ = out_ref.shape
     radial = depth_j * LANES
     half = depth_j // 2
     rows = azim * half * depth
     count = cells_ref.shape[1]
     cell = cells_ref[...]
-    a = cell // (depth * radial)
-    z = (cell // radial) % depth
-    i = cell % radial
-    lane = i // depth_j
-    j = i % depth_j
-    high = (a * half + j // 2) * depth + z
-    low = (j % 2) * LANES + lane
+    a = cell >> log2(depth * radial)
+    z = (cell >> log2(radial)) & (depth - 1)
+    i = cell & (radial - 1)
+    lane = i >> log2(depth_j)
+    j = i & (depth_j - 1)
+    high = (a * half + (j >> 1)) * depth + z
+    low = (j & 1) * LANES + lane
     chunk = 1024
-    totals = [jnp.zeros((rows, 2 * LANES), F32) for _ in range(sources)]
+    total = jnp.zeros((2 * sources * rows, 2 * LANES), F32)
     for start in range(0, count, chunk):
         at = slice(start, start + chunk)
         hot_low = jnp.where(
             lax.broadcasted_iota(jnp.int32, (2 * LANES, chunk), 0) == low[:, at], 1.0, 0.0
         ).astype(BF16)
         hit = lax.broadcasted_iota(jnp.int32, (rows, chunk), 0) == high[:, at]
+        left = []
         for s in range(sources):
             for part in pieces(weights_ref[s, :, at], 2):
-                left = jnp.where(hit, part.astype(F32), 0.0).astype(BF16)
-                totals[s] = totals[s] + lax.dot_general(
-                    left, hot_low, NT, preferred_element_type=F32
-                )
+                left.append(jnp.where(hit, part.astype(F32), 0.0).astype(BF16))
+        total = total + lax.dot_general(
+            jnp.concatenate(left, axis=0), hot_low, NT, preferred_element_type=F32
+        )
     for s in range(sources):
-        grid = totals[s].reshape(azim, half, depth, 2 * LANES)
+        first = 2 * s * rows
+        both = total[first:first + rows] + total[first + rows:first + 2 * rows]
+        grid = both.reshape(azim, half, depth, 2 * LANES)
         for jh in range(half):
             for jl in range(2):
                 out_ref[:, s, 2 * jh + jl] = grid[:, jh, :, jl * LANES:(jl + 1) * LANES]
@@ -80,16 +88,16 @@
 def order(size):
     j = size // LANES
     row = lax.broadcasted_iota(jnp.int32, (size, size), 0)
-    col = lax.broadcasted_iota(jnp.int32, (size, size), 1)
-    return jnp.where(row == (col % LANES) * j + col // LANES, 1.0, 0.0).astype(BF16)
+    col = lax.broadcasted_iota(jnp.int32, (8, size), 1)
+    want = ((col & (LANES - 1)) * j + (col >> log2(LANES)))[0:1]
+    return jnp.where(row == want, 1.0, 0.0).astype(BF16)
 
 
 def reorder(rows, matrix, dims):
-    total = None
-    for part in pieces(rows, 3):
-        term = lax.dot_general(part, matrix, dims, preferred_element_type=F32)
-        total = term if total is None else total + term
-    return total
+    count = rows.shape[0]
+    stacked = jnp.concatenate(pieces(rows, 3), axis=0)
+    out = lax.dot_general(stacked, matrix, dims, preferred_element_type=F32)
+    return out[:count] + out[count:2 * count] + out[2 * count:]
 
 
 def radius(j, inner, spacing):
@@ -228,7 +236,7 @@
     lax.fori_loop(lo, hi, body, 0)
 
 
-def kernel(ring, inner, theta, forward_ref, sig0_ref, sig1_ref, sig2_ref, b_ref, adj_ref, grad_ref,
+def kernel(ring, inner, theta, forward_ref, sig0_ref, sig1_ref, sig2_ref, cells_ref, weights_ref, adj_ref, grad_ref,
            raw0, raw1, raw2, uedge, *rest):
     rest = list(rest)
     refs = [[rest.pop(0) for _ in range(6)] for _ in range(3)]
@@ -272,14 +280,13 @@
     for k in range(1, 6):
         got_sigma.append(send(sig2_ref, raw2.at[5 - k:6 - k], k))
         got_sigma.append(send(sig2_ref, raw2.at[5 + k:6 + k], -k))
-    got_b = [send(b_ref.at[2:4], B.at[2:4], 1), send(b_ref.at[0:2], B.at[8:10], -1)]
-    got_b_far = [send(b_ref.at[1:2], B.at[1:2], 1), send(b_ref.at[2:3], B.at[10:11], -1)]
     got_u = [send(forward_ref.at[:, 3:4], uedge.at[0], 1), send(forward_ref.at[:, 0:1], uedge.at[1], -1)]
 
     raw0[4:8] = sig0_ref[...]
     raw1[4:6] = sig1_ref[...]
     raw2[5:6] = sig2_ref[...]
-    B[4:8] = b_ref[...]
+    scatter(cells_ref, weights_ref, B.at[4:8])
+    got_b = [send(B.at[6:8], B.at[2:4], 1), send(B.at[4:6], B.at[8:10], -1)]
     wide[...] = order(size)
     mid_order = order(size // 2)
     coarse_order = order(size // 4)
@@ -327,6 +334,7 @@
         return ME
 
     arrived(got_b)
+    got_b_far = [send(B.at[5:6], B.at[1:2], 1), send(B.at[6:7], B.at[10:11], -1)]
     fine.first(B, VA, 2, 10)
     fine.sweep(VA, VB, B, 3, 9)
     fix = correction(VB, cyc[0])
@@ -402,14 +410,6 @@
     theta = 2.0 * math.pi / total_azim
     j = size // LANES
     vmem = pl.BlockSpec(memory_space=pltpu.VMEM)
-    source = pl.pallas_call(
-        scatter_kernel,
-        out_shape=jax.ShapeDtypeStruct((azim, sources, j, depth, LANES), F32),
-        in_specs=[vmem] * 2,
-        out_specs=vmem,
-        compiler_params=pltpu.CompilerParams(vmem_limit_bytes=48 * 1024 * 1024),
-    )(receiver_cells, receiver_weights)
-
     def field(cells, groups, level_j):
         return pltpu.VMEM((cells, groups, level_j, 8, LANES), F32)
 
@@ -437,12 +437,12 @@
             jax.ShapeDtypeStruct((sources, azim, depth, size), F32),
             jax.ShapeDtypeStruct((azim, depth, size), F32),
         ),
-        in_specs=[vmem] * 5,
+        in_specs=[vmem] * 6,
         out_specs=(vmem, vmem),
         scratch_shapes=scratch,
         compiler_params=pltpu.CompilerParams(
             collective_id=0, has_side_effects=True, vmem_limit_bytes=48 * 1024 * 1024),
-    )(forward_field, conductivity, conductivity_mid, conductivity_coarse, source)
+    )(forward_field, conductivity, conductivity_mid, conductivity_coarse, receiver_cells, receiver_weights)
 
 
 def solution(mesh):

time: 80.7 us -> 75.9 us (0.941)
  Pallas kernels: 75.8 us -> 68.5 us
  local copies, waits for them, and re-layouts: 3.91 us -> 6.34 us
    pallas_call x1 -> x0, Pallas kernels: 5.47 us -> none  [local(): pl.pallas_call(scatter_kernel, out_shape=jax.ShapeDtypeStruct((azim, sour...]
    unnamed x14, local copies, waits for them, and re-layouts: 3.91 us -> 6.34 us
    pallas_call x1, Pallas kernels: 70.4 us -> 68.5 us  [local(): pl.pallas_call(functools.partial(kernel, ring, inner, theta), out_shape=(...]
where the time goes in v2:
time: 75.9 us; the launch traced here: 75.5 us
  Pallas kernels  68.5 us (90%)
  local copies, waits for them, and re-layouts  6.34 us (8%)
    pallas_call x1, Pallas kernels, local(): pl.pallas_call(functools.partial(kernel, ring, inner, theta), out_shape=(...  68.5 us
    unnamed x14, local copies, waits for them, and re-layouts  6.34 us

profile of v2, /device:TPU:0, one launch (start us, length us, event | category | flops | bytes accessed | tf_op | source)
XLA Modules:
  0.0 75.5 jit_solution(4828140365572473007)
XLA Ops:
  0.6 0.0 copy-start
  0.6 1.0 %copy-done = f32[4,4,8,1024]{3,2,1,0:T(8,128)S(1)} copy-done((f32[4,4,8,1024]{3,2,1,0:T(8,128)S(1)}, f32[4,4,8,1024]{3,2,1,0:T(8,128)}, u32[]{:S(2)}) %copy-start) | copy-done | bytes 524312
  1.7 0.0 copy-start.1
  1.7 0.9 %copy-done.1 = f32[4,8,1024]{2,1,0:T(8,128)S(1)} copy-done((f32[4,8,1024]{2,1,0:T(8,128)S(1)}, f32[4,8,1024]{2,1,0:T(8,128)}, u32[]{:S(2)}) %copy-start.1) | copy-done | bytes 131096
  2.6 0.0 copy-start.2
  2.6 0.8 %copy-done.2 = f32[4,1,4096]{2,1,0:T(1,128)S(1)} copy-done((f32[4,1,4096]{2,1,0:T(1,128)S(1)}, f32[4,1,4096]{2,1,0:T(1,128)}, u32[]{:S(2)}) %copy-start.2) | copy-done | bytes 65560
  3.4 0.0 copy-start.3
  3.4 0.7 copy-done.3
  4.1 0.0 copy-start.4
  4.1 0.7 copy-done.4
  4.9 0.0 copy-start.5
  4.9 0.7 copy-done.5
  5.5 68.5 %shard_map.77 = (f32[4,4,8,1024]{3,2,1,0:T(8,128)S(1)}, f32[4,8,1024]{2,1,0:T(8,128)S(1)}) custom-call(f32[4,4,8,1024]{3,2,1,0:T(8,128)S(1)} %copy-done, f32[4,8,1024]{2,1,0:T(8,128)S(1)} %copy-done.1, f32[2,4,512]{2,1,0:T(4,128)S(1)} %copy-done.3, f32[1,2,256]{2,1,0:T(2,128)S(1)} %copy-done.5, s32[1,4096]{1,0:T(1,128)S(1)} %copy-done.4, ...), custom_call_target="tpu_custom_call" | custom-call | tf_op jit(solution)/shard_map/pallas_call | solution.py:434
  74.0 0.8 %copy.10 = f32[4,4,8,1024]{3,2,1,0:T(8,128)} copy(f32[4,4,8,1024]{3,2,1,0:T(8,128)S(1)} %get-tuple-element.4) | data formatting | bytes 1048576
  74.8 0.7 copy.11
Async XLA Ops:
  0.6 1.0 %copy-start = (f32[4,4,8,1024]{3,2,1,0:T(8,128)S(1)}, f32[4,4,8,1024]{3,2,1,0:T(8,128)}, u32[]{:S(2)}) copy-start(f32[4,4,8,1024]{3,2,1,0:T(8,128)} %forward_ref.1) | copy-start | bytes 1572868
  1.7 0.9 %copy-start.1 = (f32[4,8,1024]{2,1,0:T(8,128)S(1)}, f32[4,8,1024]{2,1,0:T(8,128)}, u32[]{:S(2)}) copy-start(f32[4,8,1024]{2,1,0:T(8,128)} %sig0_ref.1) | copy-start | bytes 393220
  2.6 0.8 %copy-start.2 = (f32[4,1,4096]{2,1,0:T(1,128)S(1)}, f32[4,1,4096]{2,1,0:T(1,128)}, u32[]{:S(2)}) copy-start(f32[4,1,4096]{2,1,0:T(1,128)} %weights_ref.1) | copy-start | bytes 196612
  3.4 0.7 copy-start.3
  4.1 0.7 copy-start.4
  4.9 0.7 copy-start.5
